TPU v7x, 32 devices: a whole 2x2x4 slice. The times are simulated.
32 devices in a mesh: rep: 4 (over y, core), dp: 8 (over z, x).
Axes of the slice: x: 2, y: 2, z: 4, core: 2. Of those that a mesh axis runs over, the one named last changes fastest.
Arguments:
- first_core: float32 [512, 512], P('dp'), may hold values from -6 to 6
- first_moment: float32 [512, 512], P('dp'), may hold values from -4 to 4
- first_second: float32 [512, 512], P('dp'), may hold values from 0.01 to 1
- mid_core: float32 [256, 131072], P('dp'), may hold values from -0.5 to 0.5
- mid_moment: float32 [256, 131072], P('dp'), may hold values from -4 to 4
- mid_second: float32 [256, 131072], P('dp'), may hold values from 0.01 to 1
- last_core: float32 [512, 512], P('dp'), may hold values from -0.5 to 0.5
- last_moment: float32 [512, 512], P('dp'), may hold values from -4 to 4
- last_second: float32 [512, 512], P('dp'), may hold values from 0.01 to 1
- cotangent: bfloat16 [512, 128], P(('rep', 'dp')), may hold values from -6 to 6
- bag_lengths: int32 [32, 16], P(('rep', 'dp')), may hold values from 1 to 32, 256 in all within a row
- first_digit: int32 [8192], P(('rep', 'dp')), may hold values from 0 to 511
- mid_digit: int32 [8192, 1], P(('rep', 'dp')), may hold values from 0 to 255; in each aligned block of 256 rows (0 to 255, 256 to 511, ...) at most 2 rows name the same one
- last_digit: int32 [8192], P(('rep', 'dp')), may hold values from 0 to 511
Outputs:
- first_core_next: float32 [512, 512], P('dp')
- first_moment_next: float32 [512, 512], P('dp')
- first_second_next: float32 [512, 512], P('dp')
- mid_core_next: float32 [256, 131072], P('dp')
- mid_moment_next: float32 [256, 131072], P('dp')
- mid_second_next: float32 [256, 131072], P('dp')
- last_core_next: float32 [512, 512], P('dp')
- last_moment_next: float32 [512, 512], P('dp')
- last_second_next: float32 [512, 512], P('dp')
Inputs may be any that keep to these rules, and one draw needn't show every extreme that they name: `mid_digit`: within each block of 256 lookups no middle digit appears more than 2 times, and in some block one digit appears exactly 2 times. `bag_lengths`: each row sums to 256; some entry of each row equals 32.
All inputs are finite; a program needn't handle non-finite values.
Results may differ from a plain program's by a relative error of at most 0.0056.
Values may be sent and summed in bfloat16 or wider, within the bound.
A program may use at most 192 MiB of HBM per device.

v0:
```python
from functools import partial

import jax
import jax.numpy as jnp
from jax import lax
from jax.sharding import PartitionSpec as P

N2 = 256
N3 = 512
R = 128
D1 = 4
D2 = 8
D3 = 4
STEP = 20
CAP = 2


LEARN_RATE = 0.01
BETA_ONE = 0.9
BETA_TWO = 0.999
EPSILON = 1e-08


def adam_update(current, moment, second, gradient):
    moment_next = BETA_ONE * moment + (1.0 - BETA_ONE) * gradient
    second_next = BETA_TWO * second + (1.0 - BETA_TWO) * gradient * gradient
    corrected = moment_next / (1.0 - BETA_ONE**STEP)
    spread = jnp.sqrt(second_next / (1.0 - BETA_TWO**STEP))
    return (current - LEARN_RATE * corrected / (spread + EPSILON), moment_next, second_next)


def slot_terms(row_items, first_copy, last_copy):
    slot_grads, slot_pairs, mid_row = row_items
    slot_count = slot_grads.shape[0]
    tail_rows = last_copy.shape[0]
    grad_cube = slot_grads.reshape(slot_count, D1, D2, D3)
    first_rows = first_copy[slot_pairs // tail_rows].reshape(slot_count, D1, R)
    last_rows = last_copy[slot_pairs % tail_rows].reshape(slot_count, R, D3)
    mid_cube = mid_row.reshape(R, D2, R)
    first_mix = jnp.einsum(
        "kar,kabc->krbc", first_rows, grad_cube, preferred_element_type=jnp.float32
    ).astype(jnp.bfloat16)
    mid_term = jnp.einsum("krbc,ksc->rbs", first_mix, last_rows, preferred_element_type=jnp.float32)
    tail_mix = jnp.einsum(
        "rbs,ksc->krbc", mid_cube, last_rows, preferred_element_type=jnp.float32
    ).astype(jnp.bfloat16)
    first_term = jnp.einsum(
        "kabc,krbc->kar", grad_cube, tail_mix, preferred_element_type=jnp.float32
    )
    head_mix = jnp.einsum(
        "kar,rbs->kabs", first_rows, mid_cube, preferred_element_type=jnp.float32
    ).astype(jnp.bfloat16)
    last_term = jnp.einsum(
        "kabs,kabc->ksc", head_mix, grad_cube, preferred_element_type=jnp.float32
    )
    return (
        mid_term.reshape(-1),
        first_term.reshape(slot_count, D1 * R),
        last_term.reshape(slot_count, R * D3),
    )


def core_terms(slot_grads, slot_pairs, mid_copy, first_copy, last_copy):
    per_row = lax.map(
        partial(slot_terms, first_copy=first_copy, last_copy=last_copy),
        (slot_grads, slot_pairs, mid_copy),
    )
    mid_part, first_terms, last_terms = per_row
    tail_rows = last_copy.shape[0]
    flat_pairs = slot_pairs.reshape(-1)
    first_part = jax.ops.segment_sum(
        first_terms.reshape(-1, first_terms.shape[-1]),
        flat_pairs // tail_rows,
        num_segments=first_copy.shape[0],
    )
    last_part = jax.ops.segment_sum(
        last_terms.reshape(-1, last_terms.shape[-1]), flat_pairs % tail_rows, num_segments=tail_rows
    )
    return (mid_part, first_part, last_part)


def regroup(dense_part, dp_count, rep_count):
    column_count = dense_part.shape[1]
    grouped = dense_part.reshape(dp_count, rep_count, -1, column_count)
    return grouped.transpose(1, 0, 2, 3).reshape(-1, column_count)


def local(
    first_core,
    first_moment,
    first_second,
    mid_core,
    mid_moment,
    mid_second,
    last_core,
    last_moment,
    last_second,
    cotangent,
    bag_lengths,
    first_digit,
    mid_digit,
    last_digit,
):
    dp_count = lax.axis_size("dp")
    rep_count = lax.axis_size("rep")
    local_rows = mid_core.shape[0]
    look_count = first_digit.shape[0]
    embed_dim = cotangent.shape[1]
    positions = jnp.arange(look_count, dtype=jnp.int32)
    bag_ends = jnp.cumsum(bag_lengths[0])
    sample_of = jnp.sum((bag_ends[None, :] <= positions[:, None]).astype(jnp.int32), axis=1)
    mid_rows = mid_digit[:, 0]
    earlier = (mid_rows[None, :] == mid_rows[:, None]) & (positions[None, :] < positions[:, None])
    slot_index = mid_rows * CAP + jnp.sum(earlier.astype(jnp.int32), axis=1)
    payload = (
        jnp.zeros((N2 * CAP, embed_dim), jnp.bfloat16).at[slot_index].set(cotangent[sample_of])
    )
    pair_ids = jnp.zeros((N2 * CAP,), jnp.int32).at[slot_index].set(first_digit * N3 + last_digit)
    first_copy, last_copy = (
        lax.all_gather(first_core.astype(jnp.bfloat16), "dp", axis=0, tiled=True),
        lax.all_gather(last_core.astype(jnp.bfloat16), "dp", axis=0, tiled=True),
    )
    mid_copy = mid_core.astype(jnp.bfloat16)
    sub_rows = local_rows // rep_count
    payload = payload.reshape(dp_count, rep_count, sub_rows, CAP, embed_dim)
    pair_ids = pair_ids.reshape(dp_count, rep_count, sub_rows, CAP)
    arrived, arrived_ids = (
        lax.all_to_all(
            lax.all_to_all(payload, "rep", split_axis=1, concat_axis=3, tiled=True),
            "dp",
            split_axis=0,
            concat_axis=3,
            tiled=True,
        ),
        lax.all_to_all(
            lax.all_to_all(pair_ids, "rep", split_axis=1, concat_axis=3, tiled=True),
            "dp",
            split_axis=0,
            concat_axis=3,
            tiled=True,
        ),
    )
    own_rows = lax.dynamic_slice_in_dim(mid_copy, lax.axis_index("rep") * sub_rows, sub_rows, 0)
    mid_part, first_part, last_part = core_terms(
        arrived[0, 0], arrived_ids[0, 0], own_rows, first_copy, last_copy
    )
    mid_grad = lax.all_gather(mid_part, "rep", axis=0, tiled=True)
    pieces = (
        lax.psum_scatter(
            regroup(first_part, dp_count, rep_count), ("rep", "dp"), scatter_dimension=0, tiled=True
        ),
        lax.psum_scatter(
            regroup(last_part, dp_count, rep_count), ("rep", "dp"), scatter_dimension=0, tiled=True
        ),
    )
    first_grad, last_grad = (
        lax.all_gather(pieces[0], "rep", axis=0, tiled=True),
        lax.all_gather(pieces[1], "rep", axis=0, tiled=True),
    )
    first_next = adam_update(first_core, first_moment, first_second, first_grad)
    mid_next = adam_update(mid_core, mid_moment, mid_second, mid_grad)
    last_next = adam_update(last_core, last_moment, last_second, last_grad)
    return (
        first_next[0],
        first_next[1],
        first_next[2],
        mid_next[0],
        mid_next[1],
        mid_next[2],
        last_next[0],
        last_next[1],
        last_next[2],
    )


def solution(mesh):
    return jax.shard_map(
        local,
        mesh=mesh,
        in_specs=(
            P("dp", None),
            P("dp", None),
            P("dp", None),
            P("dp", None),
            P("dp", None),
            P("dp", None),
            P("dp", None),
            P("dp", None),
            P("dp", None),
            P(("rep", "dp"), None),
            P(("rep", "dp"), None),
            P(("rep", "dp")),
            P(("rep", "dp"), None),
            P(("rep", "dp")),
        ),
        out_specs=(
            P("dp", None),
            P("dp", None),
            P("dp", None),
            P("dp", None),
            P("dp", None),
            P("dp", None),
            P("dp", None),
            P("dp", None),
            P("dp", None),
        ),
        check_vma=False,
    )
```

profile of v0, /device:TPU:0, one launch (start us, length us, event | category | flops | bytes accessed | tf_op | source)
XLA Modules:
  0.0 651.3 jit_solution(10973549176045945165)
XLA Ops:
  8.0 0.9 convert_reduce_fusion
  10.3 1.4 scatter_custom_fusion
  12.8 4.2 all-to-all-start
  19.0 32.2 %all_gather.16 = bf16[512,512]{1,0:T(8,128)(2,1)S(1)} all-gather(bf16[64,512]{1,0:T(8,128)(2,1)S(1)} %convert_element_type.39), channel_id=1, replica_groups=mesh['rep'=4,'dp'=8] {'dp'}, dimensions={0}, use_global_device_ids=true | all-gather | bytes 589824 | tf_op jit(solution)/shard_map/all_gather | solution.py:121
  51.1 3.7 dynamic-slice_convert_fusion
  56.7 5.5 all-to-all-start.1
  63.2 1.8 scatter_custom_fusion.1
  65.8 3.2 all-to-all-done.1
  69.0 3.3 all-to-all-start.2
  72.3 31.6 %all_gather.15 = bf16[512,512]{1,0:T(8,128)(2,1)S(1)} all-gather(bf16[64,512]{1,0:T(8,128)(2,1)S(1)} %convert_element_type.37), channel_id=1, replica_groups=mesh['rep'=4,'dp'=8] {'dp'}, dimensions={0}, use_global_device_ids=true | all-gather | bytes 589824 | tf_op jit(solution)/shard_map/all_gather | solution.py:120
  104.8 3.4 all-to-all-start.3
  108.5 6.9 %all-to-all-done.3 = bf16[8,1,8,8,128]{4,2,3,1,0:T(8,128)(2,1)S(1)} async-done(((bf16[8,1,8,8,128]{4,2,3,1,0:T(8,128)(2,1)}), bf16[8,1,8,8,128]{4,2,3,1,0:T(8,128)(2,1)S(1)}, u32[]{:S(2)}, u32[]{:S(2)}) %all-to-all-start.3) | async-done | bytes 131104 | tf_op jit(solution)/shard_map/all_to_all | solution.py:128
  116.1 203.2 %while.16 = (s32[]{:T(128)}, f32[8,131072]{1,0:T(8,128)}, f32[8,64,512]{2,1,0:T(8,128)}, f32[8,64,512]{2,1,0:T(8,128)}, s32[8,64]{1,0:T(8,128)S(1)}, /*index=5*/...) while((s32[]{:T(128)}, f32[8,131072]{1,0:T(8,128)}, ...), condition=%wide.region_6.7_spmd, body=%wide.region_5.6_spmd.sunk | while | flops 208408384 | bytes 10676877 | solution.py:64
  119.3 3.2 dynamic-slice_reduce_fusion.2
  123.9 1.7 copy.162
  126.4 2.0 copy.168
  128.4 1.4 convolution_bitcast_fusion.5
  130.7 10.8 %dynamic_update_slice.25 = f32[8,131072]{1,0:T(8,128)} dynamic-update-slice(f32[8,131072]{1,0:T(8,128)} %get-tuple-element.274, f32[1,131072]{1,0:T(1,128)S(1)} %bitcast.139, s32[]{:T(128)S(6)} %copy.176, s32[]{:T(128)} %constant.135.clone.1..sunk) | dynamic-update-slice | bytes 1048580 | tf_op jit(solution)/shard_map/while/body/jit(dynamic_update_index_in_dim)/dynamic_update_slice | solution.py:64
  144.6 3.2 dynamic-slice_reduce_fusion.2
  149.3 1.7 copy.162
  151.8 2.0 copy.168
  153.8 1.4 convolution_bitcast_fusion.5
  156.0 10.9 %dynamic_update_slice.25 = f32[8,131072]{1,0:T(8,128)} dynamic-update-slice(f32[8,131072]{1,0:T(8,128)} %get-tuple-element.274, f32[1,131072]{1,0:T(1,128)S(1)} %bitcast.139, s32[]{:T(128)S(6)} %copy.176, s32[]{:T(128)} %constant.135.clone.1..sunk) | dynamic-update-slice | bytes 1048580 | tf_op jit(solution)/shard_map/while/body/jit(dynamic_update_index_in_dim)/dynamic_update_slice | solution.py:64
  170.1 3.2 dynamic-slice_reduce_fusion.2
  174.7 1.7 copy.162
  177.2 2.0 copy.168
  179.2 1.4 convolution_bitcast_fusion.5
  181.4 10.9 %dynamic_update_slice.25 = f32[8,131072]{1,0:T(8,128)} dynamic-update-slice(f32[8,131072]{1,0:T(8,128)} %get-tuple-element.274, f32[1,131072]{1,0:T(1,128)S(1)} %bitcast.139, s32[]{:T(128)S(6)} %copy.176, s32[]{:T(128)} %constant.135.clone.1..sunk) | dynamic-update-slice | bytes 1048580 | tf_op jit(solution)/shard_map/while/body/jit(dynamic_update_index_in_dim)/dynamic_update_slice | solution.py:64
  195.5 3.2 dynamic-slice_reduce_fusion.2
  200.1 1.7 copy.162
  202.6 2.0 copy.168
  204.6 1.4 convolution_bitcast_fusion.5
  206.8 10.9 %dynamic_update_slice.25 = f32[8,131072]{1,0:T(8,128)} dynamic-update-slice(f32[8,131072]{1,0:T(8,128)} %get-tuple-element.274, f32[1,131072]{1,0:T(1,128)S(1)} %bitcast.139, s32[]{:T(128)S(6)} %copy.176, s32[]{:T(128)} %constant.135.clone.1..sunk) | dynamic-update-slice | bytes 1048580 | tf_op jit(solution)/shard_map/while/body/jit(dynamic_update_index_in_dim)/dynamic_update_slice | solution.py:64
  220.9 3.2 dynamic-slice_reduce_fusion.2
  225.5 1.7 copy.162
  228.0 2.0 copy.168
  230.0 1.4 convolution_bitcast_fusion.5
  232.2 10.9 %dynamic_update_slice.25 = f32[8,131072]{1,0:T(8,128)} dynamic-update-slice(f32[8,131072]{1,0:T(8,128)} %get-tuple-element.274, f32[1,131072]{1,0:T(1,128)S(1)} %bitcast.139, s32[]{:T(128)S(6)} %copy.176, s32[]{:T(128)} %constant.135.clone.1..sunk) | dynamic-update-slice | bytes 1048580 | tf_op jit(solution)/shard_map/while/body/jit(dynamic_update_index_in_dim)/dynamic_update_slice | solution.py:64
  246.3 3.2 dynamic-slice_reduce_fusion.2
  250.9 1.7 copy.162
  253.4 2.0 copy.168
  255.4 1.4 convolution_bitcast_fusion.5
  257.7 10.9 %dynamic_update_slice.25 = f32[8,131072]{1,0:T(8,128)} dynamic-update-slice(f32[8,131072]{1,0:T(8,128)} %get-tuple-element.274, f32[1,131072]{1,0:T(1,128)S(1)} %bitcast.139, s32[]{:T(128)S(6)} %copy.176, s32[]{:T(128)} %constant.135.clone.1..sunk) | dynamic-update-slice | bytes 1048580 | tf_op jit(solution)/shard_map/while/body/jit(dynamic_update_index_in_dim)/dynamic_update_slice | solution.py:64
  271.7 3.2 dynamic-slice_reduce_fusion.2
  276.3 1.7 copy.162
  278.8 2.0 copy.168
  280.8 1.4 convolution_bitcast_fusion.5
  283.1 10.9 %dynamic_update_slice.25 = f32[8,131072]{1,0:T(8,128)} dynamic-update-slice(f32[8,131072]{1,0:T(8,128)} %get-tuple-element.274, f32[1,131072]{1,0:T(1,128)S(1)} %bitcast.139, s32[]{:T(128)S(6)} %copy.176, s32[]{:T(128)} %constant.135.clone.1..sunk) | dynamic-update-slice | bytes 1048580 | tf_op jit(solution)/shard_map/while/body/jit(dynamic_update_index_in_dim)/dynamic_update_slice | solution.py:64
  297.1 3.2 dynamic-slice_reduce_fusion.2
  301.7 1.7 copy.162
  304.2 2.0 copy.168
  306.2 1.4 convolution_bitcast_fusion.5
  308.5 10.9 %dynamic_update_slice.25 = f32[8,131072]{1,0:T(8,128)} dynamic-update-slice(f32[8,131072]{1,0:T(8,128)} %get-tuple-element.274, f32[1,131072]{1,0:T(1,128)S(1)} %bitcast.139, s32[]{:T(128)S(6)} %copy.176, s32[]{:T(128)} %constant.135.clone.1..sunk) | dynamic-update-slice | bytes 1048580 | tf_op jit(solution)/shard_map/while/body/jit(dynamic_update_index_in_dim)/dynamic_update_slice | solution.py:64
  319.3 4.5 scatter_custom_fusion.2
  323.8 1.0 copy.111
  325.2 4.5 scatter_custom_fusion.3
  329.7 1.0 copy.113
  331.4 128.7 %reduce-scatter.3.cloned.1.call-done = f32[16,512]{1,0:T(8,128)} async-done(((f32[512,512]{1,0:T(8,128)}), f32[16,512]{1,0:T(8,128)}) %reduce-scatter.3.cloned.1.call-update) | async-done | bytes 32784 | tf_op jit(solution)/shard_map/reduce_scatter | solution.py:149
  460.0 5.6 all_gather.17
  465.6 129.0 %reduce-scatter.5.cloned.1.call-done = f32[16,512]{1,0:T(8,128)} async-done(((f32[512,512]{1,0:T(8,128)}), f32[16,512]{1,0:T(8,128)}) %reduce-scatter.5.cloned.1.call-update) | async-done | bytes 32784 | tf_op jit(solution)/shard_map/reduce_scatter | solution.py:152
  594.6 5.6 all_gather.19
  600.3 1.8 divide_subtract_fusion.1
  602.1 1.8 divide_subtract_fusion.2
  603.9 40.0 %divide_subtract_fusion = (f32[32,131072]{1,0:T(8,128)}, f32[32,131072]{1,0:T(8,128)}, f32[32,131072]{1,0:T(8,128)}) fusion(f32[32,131072]{1,0:T(8,128)} %param.19, f32[32,131072]{1,0:T(8,128)} %all-gather.2.cloned.1.call-done, f32[32,131072]{1,0:T(8,128)} %param.20, f32[32,131072]{1,0:T(8,128)} %param.21), kind=kLoop, calls=%fused_computation.41 | loop fusion | flops 50331648 | bytes 117440512 | tf_op jit(solution)/shard_map/sub | solution.py:29
  (225 shorter events, 58.9 us)
Async XLA Ops:
  8.0 55.2 %copy-start = (bf16[16,128]{1,0:T(8,128)(2,1)S(1)}, bf16[16,128]{1,0:T(8,128)(2,1)}, u32[]{:S(2)}) copy-start(bf16[16,128]{1,0:T(8,128)(2,1)} %param.25) | copy-start | bytes 12292
  12.8 42.0 %all-to-all-start = ((s32[4,1,128]{2,1,0:T(1,128)}), s32[4,1,128]{2,1,0:T(1,128)S(1)}, u32[]{:S(2)}, u32[]{:S(2)}) async-start(s32[4,1,128]{2,1,0:T(1,128)} %reshape.443), calls=%async_computation | async-start | bytes 4096 | tf_op jit(solution)/shard_map/all_to_all | solution.py:136
  56.7 12.2 %all-to-all-start.1 = ((s32[8,1,8,8]{2,3,1,0:T(8,128)}), s32[8,1,8,8]{2,3,1,0:T(8,128)S(1)}, u32[]{:S(2)}, u32[]{:S(2)}) async-start(s32[8,1,8,8]{2,3,1,0:T(8,128)} %copy.101), calls=%async_computation.1 | async-start | bytes 65536 | tf_op jit(solution)/shard_map/all_to_all | solution.py:135
  69.0 35.1 %all-to-all-start.2 = ((bf16[8,4,8,2,128]{4,3,2,0,1:T(2,128)(2,1)}), bf16[8,4,8,2,128]{4,3,2,0,1:T(2,128)(2,1)S(1)}, u32[]{:S(2)}, u32[]{:S(2)}) async-start(bf16[8,4,8,2,128]{4,3,2,0,1:T(2,128)(2,1)} %copy.105), calls=%async_computation.2 | async-start | bytes 262144 | tf_op jit(solution)/shard_map/all_to_all | solution.py:129
  104.8 10.7 %all-to-all-start.3 = ((bf16[8,1,8,8,128]{4,2,3,1,0:T(8,128)(2,1)}), bf16[8,1,8,8,128]{4,2,3,1,0:T(8,128)(2,1)S(1)}, u32[]{:S(2)}, u32[]{:S(2)}) async-start(bf16[8,1,8,8,128]{4,2,3,1,0:T(8,128)(2,1)} %bitcast.36), calls=%async_computation.3 | async-start | bytes 262144 | tf_op jit(solution)/shard_map/all_to_all | solution.py:128
  108.2 351.9 %reduce-scatter.3.cloned.1.call-start = ((), (), s32[]{:S(2)}) async-start(), calls=%async_computation.6 | async-start | bytes 1081344 | tf_op jit(solution)/shard_map/reduce_scatter | solution.py:149
  324.9 269.7 %reduce-scatter.5.cloned.1.call-start = ((), (), s32[]{:S(2)}) async-start(), calls=%async_computation.8 | async-start | bytes 1081344 | tf_op jit(solution)/shard_map/reduce_scatter | solution.py:152
  330.8 273.1 %all-gather.2.cloned.1.call-start = ((), (), s32[]{:S(2)}) async-start(), calls=%async_computation.7 | async-start | bytes 20971520 | tf_op jit(solution)/shard_map/all_gather | solution.py:147
  603.9 40.0 %copy-start.1 = (bf16[16,128]{1,0:T(8,128)(2,1)S(1)}, bf16[16,128]{1,0:T(8,128)(2,1)}, u32[]{:S(2)}) copy-start(bf16[16,128]{1,0:T(8,128)(2,1)} %param.25) | copy-start | bytes 12292
Sparse Core Ops, SparseCore 0:
  325.0 134.9 reduce-scatter.2
  462.9 131.6 reduce-scatter.4
Sparse Core Ops, SparseCore 1:
  333.5 107.7 all-gather.1
where the time goes:
time: 655 us; the launch traced here: 651 us
  waiting for transfers between devices  268 us (41%)
  local copies, waits for them, and re-layouts  190 us (29%)
  blocking collectives  75 us (11%)
  other arithmetic  58 us (9%)
  matrix products  26.5 us (4%)
  starting transfers between devices  17 us (3%)
  between operations  15.6 us (2%)
    reduce_scatter x1, waiting for transfers between devices, local(): lax.psum_scatter(regroup(last_part, dp_count, rep_count), ('rep', 'dp'),...  129 us
    reduce_scatter x1, waiting for transfers between devices, local(): lax.psum_scatter(regroup(first_part, dp_count, rep_count), ('rep', 'dp'),...  129 us
    dynamic_update_slice x24, local copies, waits for them, and re-layouts, core_terms(): lax.map(partial(slot_terms, first_copy=first_copy, last_copy=last_copy),...  93.6 us
    sub x3, other arithmetic, adam_update(): current - LEARN_RATE * corrected / (spread + EPSILON)  43.6 us
    dynamic_slice x24, local copies, waits for them, and re-layouts, core_terms(): lax.map(partial(slot_terms, first_copy=first_copy, last_copy=last_copy),...  32.4 us
    all_gather x1, blocking collectives, local(): lax.all_gather(last_core.astype(jnp.bfloat16), 'dp', axis=0, tiled=True)  32.2 us
    all_gather x1, blocking collectives, local(): lax.all_gather(first_core.astype(jnp.bfloat16), 'dp', axis=0, tiled=True)  31.6 us
    convert_element_type x8, local copies, waits for them, and re-layouts, slot_terms(): tail_mix = jnp.einsum('rbs,ksc->krbc', mid_cube, last_rows, preferred_ele...  16 us
  transfers between devices with their start and end apart: 7, of which 4 were waited for; matrix products, arithmetic and copies ran while one was open for 3% of the time, Pallas kernels for 0%

commit v1 on v0

v1 whole, which is shorter than its diff:
```python
import jax
import jax.numpy as jnp
from jax import lax
from jax.experimental import pallas as pl
from jax.experimental.pallas import tpu as pltpu
from jax.sharding import PartitionSpec as P

R = 128
D1 = 4
D2 = 8
D3 = 4
STEP = 20
CAP = 2
GROUP_ROWS = 8
RCHUNK = 16
LANES = RCHUNK * D2

LEARN_RATE = 0.01
BETA_ONE = 0.9
BETA_TWO = 0.999
EPSILON = 1e-08

F32 = jnp.float32
BF16 = jnp.bfloat16


def adam_update(current, moment, second, gradient):
    moment_next = BETA_ONE * moment + (1.0 - BETA_ONE) * gradient
    second_next = BETA_TWO * second + (1.0 - BETA_TWO) * gradient * gradient
    corrected = moment_next * (LEARN_RATE / (1.0 - BETA_ONE**STEP))
    spread = jnp.sqrt(second_next * (1.0 / (1.0 - BETA_TWO**STEP)))
    return (current - corrected / (spread + EPSILON), moment_next, second_next)


def contract(left, right, left_dim, right_dim):
    return lax.dot_general(
        left, right, (((left_dim,), (right_dim,)), ((), ())), preferred_element_type=F32
    )


def mid_kernel(group, slots, part_ref, g_ref, f_ref, l_ref, core_ref, moment_ref, second_ref,
               core_out, moment_out, second_out, first_out, last_out,
               grad_wide, first_wide, mix, core_rows, grad_rows, first_wide_terms):
    chunk = pl.program_id(1)
    part = part_ref[0]
    row_id = lax.broadcasted_iota(jnp.int32, (R, LANES), 0)
    lane_id = lax.broadcasted_iota(jnp.int32, (R, LANES), 1)

    @pl.when(chunk == 0)
    def _():
        grads = g_ref[...]
        for a in range(D1):
            for c in range(D3):
                spread = (row_id == a * D2 * D3 + (lane_id % D2) * D3 + c).astype(F32).astype(BF16)
                grad_wide[a * D3 + c] = contract(grads, spread, 1, 0).astype(BF16)
        first_out[...] = jnp.zeros_like(first_out)
        last_out[...] = jnp.zeros_like(last_out)

    for tile in range(LANES):
        core_rows[tile * group:(tile + 1) * group, :] = core_ref[:, tile * R:(tile + 1) * R]
    pick = (row_id == chunk * RCHUNK + lane_id // D2).astype(F32).astype(BF16)
    for a in range(D1):
        first_wide[a] = contract(f_ref[:, a * R:(a + 1) * R], pick, 1, 0)

    for row in range(group):
        own = slice(row * slots, (row + 1) * slots)
        for c in range(D3):
            total = first_wide[0, own] * grad_wide[c, own].astype(F32)
            for a in range(1, D1):
                total += first_wide[a, own] * grad_wide[a * D3 + c, own].astype(F32)
            mix[row, c] = total.astype(BF16)
        first_mix = mix[row].reshape(D3 * slots, LANES)
        last_rows = jnp.concatenate(
            [l_ref[own, c * R:(c + 1) * R] for c in range(D3)], axis=0
        )
        grad_rows[pl.ds(row, LANES, stride=group), :] = contract(first_mix, last_rows, 0, 0)
        core_row = core_rows[pl.ds(row, LANES, stride=group), :].astype(BF16)
        tail = contract(last_rows, core_row, 1, 1)
        terms = grad_wide[part * D3, own].astype(F32) * tail[:slots]
        for c in range(1, D3):
            terms += (
                grad_wide[part * D3 + c, own].astype(F32) * tail[c * slots:(c + 1) * slots]
            )
        first_wide_terms[own, :] = terms.astype(BF16)
        last_out[own, :] += contract(mix[row, part], core_row, 1, 0)
    first_out[...] += contract(first_wide_terms[...], pick, 1, 1)

    for tile in range(LANES):
        cols = slice(tile * R, (tile + 1) * R)
        core_next, moment_next, second_next = adam_update(
            core_ref[:, cols], moment_ref[:, cols], second_ref[:, cols],
            grad_rows[tile * group:(tile + 1) * group, :],
        )
        core_out[:, cols] = core_next
        moment_out[:, cols] = moment_next
        second_out[:, cols] = second_next


def mid_step(part, grads, firsts, lasts, core, moment, second):
    rows, columns = core.shape
    slots = grads.shape[0] // rows
    group = min(GROUP_ROWS, rows)
    held = group * slots
    chunks = R // RCHUNK
    state = pl.BlockSpec((group, RCHUNK * D2 * R), lambda g, j: (g, j))
    terms = pl.BlockSpec((held, R), lambda g, j: (g, 0))
    wide = pl.BlockSpec((held, D1 * R), lambda g, j: (g, 0))
    return pl.pallas_call(
        lambda *refs: mid_kernel(group, slots, *refs),
        grid=(rows // group, chunks),
        in_specs=[
            pl.BlockSpec(memory_space=pltpu.SMEM), terms, wide, wide, state, state, state,
        ],
        out_specs=[state, state, state, terms, terms],
        out_shape=[jax.ShapeDtypeStruct((rows, columns), F32)] * 3
        + [jax.ShapeDtypeStruct((rows * slots, R), F32)] * 2,
        scratch_shapes=[
            pltpu.VMEM((D1 * D3, held, LANES), BF16),
            pltpu.VMEM((D1, held, LANES), F32),
            pltpu.VMEM((group, D3, slots, LANES), BF16),
            pltpu.VMEM((LANES * group, R), F32),
            pltpu.VMEM((LANES * group, R), F32),
            pltpu.VMEM((held, LANES), BF16),
        ],
        compiler_params=pltpu.CompilerParams(vmem_limit_bytes=56 * 1024 * 1024),
    )(part, grads, firsts, lasts, core, moment, second)


def local(
    first_core, first_moment, first_second,
    mid_core, mid_moment, mid_second,
    last_core, last_moment, last_second,
    cotangent, bag_lengths, first_digit, mid_digit, last_digit,
):
    dp_count = lax.axis_size("dp")
    rep_count = lax.axis_size("rep")
    local_rows = mid_core.shape[0]
    block_samples, embed_dim = cotangent.shape
    look_count = first_digit.shape[0]
    outer_rows = first_core.shape[0] * dp_count

    positions = jnp.arange(look_count, dtype=jnp.int32)
    samples = jnp.arange(block_samples, dtype=jnp.int32)
    bag_ends = jnp.sum(
        jnp.where(samples[None, :] <= samples[:, None], bag_lengths[0][None, :], 0), axis=1
    )
    sample_of = jnp.sum((bag_ends[:, None] <= positions[None, :]).astype(jnp.int32), axis=0)
    pieces = jnp.stack(
        [
            mid_digit[:, 0],
            first_digit // 2,
            last_digit // 2,
            sample_of * 4 + (first_digit % 2) * 2 + last_digit % 2,
        ]
    )
    packed = jnp.concatenate([cotangent, pieces.astype(BF16).reshape(-1, embed_dim)], axis=0)
    packed_all = lax.all_gather(packed, ("rep", "dp"), axis=0, tiled=False)

    column = jnp.arange(R * D3, dtype=jnp.int32)
    reorder = ((column[:, None] % D3) * R + column[:, None] // D3 == column[None, :]).astype(F32)
    last_wide = jnp.dot(
        last_core.astype(BF16), reorder.astype(BF16), preferred_element_type=F32
    ).astype(BF16)
    cores = lax.all_gather(
        jnp.concatenate([first_core.astype(BF16), last_wide], axis=1), "dp", axis=0, tiled=True
    )

    blocks = packed_all.shape[0]
    grads_all = packed_all[:, :block_samples].reshape(blocks * block_samples, embed_dim)
    numbers = packed_all[:, block_samples:].reshape(blocks, 4, look_count).astype(jnp.int32)
    rest = numbers[:, 3]
    keys = (
        (rest // 4) * (outer_rows * outer_rows)
        + (numbers[:, 1] * 2 + (rest // 2) % 2) * outer_rows
        + numbers[:, 2] * 2 + rest % 2
    )
    own_digits = lax.axis_index("dp") * local_rows + jnp.arange(local_rows, dtype=jnp.int32)
    match = numbers[:, 0][None] == own_digits[:, None, None]
    big = jnp.int32(2**30)
    low = jnp.min(jnp.where(match, keys[None], big), axis=2)
    high = jnp.max(jnp.where(match, keys[None], -1), axis=2)
    count = jnp.sum(match.astype(jnp.int32), axis=2)
    slot_keys = jnp.concatenate([jnp.where(count >= 1, low, -1), jnp.where(count >= 2, high, -1)], 1)
    slot_block = jnp.arange(CAP * blocks, dtype=jnp.int32) % blocks
    valid = slot_keys >= 0
    slot_keys = jnp.maximum(slot_keys, 0)
    slot_sample = jnp.where(
        valid, slot_keys // (outer_rows * outer_rows) + slot_block[None, :] * block_samples, -1
    ).reshape(-1)
    slot_first = ((slot_keys // outer_rows) % outer_rows).reshape(-1)
    slot_last = (slot_keys % outer_rows).reshape(-1)

    def one_hot(index, size):
        return (index[:, None] == jnp.arange(size, dtype=jnp.int32)[None, :]).astype(BF16)

    first_hot = one_hot(slot_first, outer_rows)
    last_hot = one_hot(slot_last, outer_rows)
    grads = jnp.dot(
        one_hot(slot_sample, blocks * block_samples), grads_all, preferred_element_type=F32
    ).astype(BF16)
    firsts = jnp.dot(first_hot, cores[:, : D1 * R], preferred_element_type=F32).astype(BF16)
    lasts = jnp.dot(last_hot, cores[:, D1 * R :], preferred_element_type=F32).astype(BF16)

    part = lax.axis_index("rep").astype(jnp.int32).reshape(1)
    core_next, moment_next, second_next, first_terms, last_terms = mid_step(
        part, grads, firsts, lasts, mid_core, mid_moment, mid_second
    )
    partial = jnp.concatenate(
        [
            contract(first_hot, first_terms.astype(BF16), 0, 0),
            contract(last_hot, last_terms.astype(BF16), 0, 0),
        ],
        axis=1,
    ).astype(BF16)
    partial = partial.reshape(dp_count, outer_rows // dp_count, 2 * R)
    arrived = lax.all_to_all(partial, "dp", split_axis=0, concat_axis=0, tiled=True)
    summed = jnp.sum(arrived.astype(F32), axis=0)
    whole = lax.all_gather(summed, "rep", axis=0, tiled=False)
    first_grad = jnp.concatenate([whole[q, :, :R] for q in range(rep_count)], axis=1)
    last_grad = lax.dot_general(
        jnp.concatenate([whole[q, :, R:] for q in range(rep_count)], axis=1),
        reorder,
        (((1,), (1,)), ((), ())),
        precision=lax.Precision.HIGHEST,
        preferred_element_type=F32,
    )
    first_next = adam_update(first_core, first_moment, first_second, first_grad)
    last_next = adam_update(last_core, last_moment, last_second, last_grad)
    return (*first_next, core_next, moment_next, second_next, *last_next)


def solution(mesh):
    core = P("dp", None)
    both = P(("rep", "dp"), None)
    return jax.shard_map(
        local,
        mesh=mesh,
        in_specs=(core,) * 9 + (both, both, P(("rep", "dp")), both, P(("rep", "dp"))),
        out_specs=(core,) * 9,
        check_vma=False,
    )
```

time: 655 us -> 190 us (0.29)
  waiting for transfers between devices: 268 us -> 0.02 us
  local copies, waits for them, and re-layouts: 190 us -> 0.8 us
  Pallas kernels: 0 us -> 61.4 us
  other arithmetic: 58 us -> 7.4 us
  starting transfers between devices: 17 us -> 0.04 us
  blocking collectives: 75 us -> 87.6 us
  matrix products: 26.5 us -> 16.4 us
    reduce_scatter x2 -> x0, waiting for transfers between devices: 258 us -> none  [the longest x1 129 us: local(): lax.psum_scatter(regroup(last_part, dp_count, rep_count), ('rep', 'dp'),...]
    dynamic_update_slice x24 -> x0, local copies, waits for them, and re-layouts: 93.6 us -> none  [core_terms(): lax.map(partial(slot_terms, first_copy=first_copy, last_copy=last_copy),...]
    pallas_call x0 -> x1, Pallas kernels: none -> 61.4 us  [mid_step(): pl.pallas_call(lambda *refs: mid_kernel(group, slots, *refs), grid=(rows...]
    sub x3 -> x1, other arithmetic: 43.6 us -> 0.79 us  [adam_update(): return (current - corrected / (spread + EPSILON), moment_next, second_next)]
    convert_element_type x17 -> x2, local copies, waits for them, and re-layouts: 33.6 us -> 0.07 us  [the longest x1 0.06 us: local(): packed_all[:, block_samples:].reshape(blocks, 4, look_count)]
    dynamic_slice x24 -> x0, local copies, waits for them, and re-layouts: 32.4 us -> none  [core_terms(): lax.map(partial(slot_terms, first_copy=first_copy, last_copy=last_copy),...]
    all_to_all x4 -> x0, starting transfers between devices: 16.5 us -> none  [the longest x1 5.53 us: local(): lax.all_to_all(lax.all_to_all(pair_ids, 'rep', split_axis=1, concat_axis=...]
    gather x24 -> x0, local copies, waits for them, and re-layouts: 12.2 us -> none  [the longest x16 6.55 us: slot_terms(): last_rows = last_copy[slot_pairs % tail_rows].reshape(slot_count, R, D3)]
  transfers between devices with their start and end apart: 7 -> 1, of which waited for: 4 -> 0; matrix products, arithmetic and copies ran while one was open for 3% -> 4% of each run, Pallas kernels for 0% -> 0%
where the time goes in v1:
time: 190 us; the launch traced here: 188 us
  blocking collectives  87.6 us (46%)
  Pallas kernels  61.4 us (32%)
  matrix products  16.4 us (9%)
  between operations  14.3 us (8%)
  other arithmetic  7.4 us (4%)
    all_gather x1, blocking collectives, local(): packed_all = lax.all_gather(packed, ('rep', 'dp'), axis=0, tiled=False)  71.2 us
    pallas_call x1, Pallas kernels, mid_step(): pl.pallas_call(lambda *refs: mid_kernel(group, slots, *refs), grid=(rows...  61.4 us
    all_to_all x1, blocking collectives, local(): lax.all_to_all(partial, 'dp', split_axis=0, concat_axis=0, tiled=True)  10.6 us
    all_gather x1, blocking collectives, local(): whole = lax.all_gather(summed, 'rep', axis=0, tiled=False)  5.79 us
    dot_general x2, matrix products, contract(): lax.dot_general(left, right, (((left_dim,), (right_dim,)), ((), ())), pre...  5.72 us
  transfers between devices with their start and end apart: 1, of which 0 were waited for; matrix products, arithmetic and copies ran while one was open for 4% of the time, Pallas kernels for 0%

profile of v1, /device:TPU:0, one launch (start us, length us, event | category | flops | bytes accessed | tf_op | source)
XLA Modules:
  0.0 187.9 jit_solution(16867628021393406012)
XLA Ops:
  7.2 0.0 all-gather.4.cloned.1.call-start
  7.2 0.9 convert_element_type.64
  8.2 1.2 fusion.15
  9.3 0.7 pad_maximum_fusion.1
  10.0 0.0 all-gather.4.cloned.1.call-update
  10.0 0.8 select_reduce_fusion
  10.8 0.1 convert_reduce_fusion.1
  10.9 0.7 fusion.63
  11.6 0.7 convert_bitcast_fusion
  12.4 0.7 pad_maximum_fusion.3
  13.1 71.2 %all-gather = bf16[768,128]{1,0:T(8,128)(2,1)S(1)} all-gather(bf16[24,128]{1,0:T(8,128)(2,1)S(1)} %pad_maximum_fusion.3), channel_id=2, replica_groups=mesh['rep'=4,'dp'=8] {'rep','dp'}, dimensions={0}, use_global_device_ids=true | all-gather | bytes 202752 | tf_op jit(solution)/shard_map/all_gather | solution.py:157
  84.3 0.1 reshape.269
  84.4 0.1 fusion.70
  84.5 0.1 add.198
  84.6 0.1 fusion.40
  84.7 1.8 fusion.17
  86.4 0.1 maximum_shift-right-logical_fusion.1
  86.5 0.1 div.90
  86.6 0.1 ne.235
  86.7 0.1 ge.27
  86.8 0.1 ne.231
  86.9 0.1 div.93
  87.0 0.1 rem.184
  87.1 1.8 fusion.7.refs_1_
  88.8 0.0 all-gather.4.cloned.1.call-done
  88.8 0.0 copy-start.3
  88.8 3.7 %fusion.5.refs_2_ = bf16[2048,512]{1,0:T(8,128)(2,1)} fusion(s32[2048]{0:T(1024)S(1)} %get-tuple-element.49, bf16[512,1024]{1,0:T(8,128)(2,1)} %all-gather.4.cloned.1.call-done), kind=kOutput, calls=%fused_computation.8 | convolution fusion | flops 1075838976 | bytes 2629632 | tf_op jit(solution)/shard_map/dot_general | solution.py:201
  92.5 0.0 copy-done.3
  92.5 2.5 %fusion.6.refs_3_ = bf16[2048,512]{1,0:T(8,128)(2,1)} fusion(s32[2048]{0:T(1024)S(1)} %get-tuple-element.50, bf16[512,1024]{1,0:T(8,128)(2,1)S(1)} %copy-done.3), kind=kOutput, calls=%fused_computation.9 | convolution fusion | flops 1075838976 | bytes 2629632 | tf_op jit(solution)/shard_map/dot_general | solution.py:202
  95.0 61.4 %shard_map.205 = (f32[32,131072]{1,0:T(8,128)}, f32[32,131072]{1,0:T(8,128)}, f32[32,131072]{1,0:T(8,128)}, f32[2048,128]{1,0:T(8,128)}, f32[2048,128]{1,0:T(8,128)}) custom-call(s32[1]{0:T(128)} %bitcast.7.refs_0_, bf16[2048,128]{1,0:T(8,128)(2,1)} %fusion.7.refs_1_, bf16[2048,512]{1,0:T(8,128)(2,1)} %fusion.5.refs_2_, bf16[2048,512]{1,0:T(8,128)(2,1)} %fusion.6.refs_3_, ...), custom_call_target="tpu_custom_call" | custom-call | tf_op jit(solution)/shard_map/pallas_call | solution.py:108
  156.4 0.0 copy-start.4
  156.4 0.0 copy-start.5
  156.4 0.0 copy-start.6
  156.4 0.0 copy-start
  156.4 0.0 copy-start.1
  156.4 0.0 copy-start.2
  156.5 2.9 %fusion.13 = bf16[512,128]{1,0:T(8,128)(2,1)S(1)} fusion(s32[2048]{0:T(1024)S(1)} %get-tuple-element.49, f32[2048,128]{1,0:T(8,128)} %get-tuple-element.14), kind=kOutput, calls=%fused_computation.19 | convolution fusion | flops 269811712 | bytes 1187840 | tf_op jit(solution)/shard_map/dot_general | solution.py:36
  159.4 2.8 %fusion.14 = bf16[512,128]{1,0:T(8,128)(2,1)S(1)} fusion(s32[2048]{0:T(1024)S(1)} %get-tuple-element.50, f32[2048,128]{1,0:T(8,128)} %get-tuple-element.15), kind=kOutput, calls=%fused_computation.20 | convolution fusion | flops 269811712 | bytes 1187840 | tf_op jit(solution)/shard_map/dot_general | solution.py:36
  162.2 10.6 %all_to_all.5 = bf16[8,64,256]{2,1,0:T(8,128)(2,1)S(1)} all-to-all(bf16[8,64,256]{2,1,0:T(8,128)(2,1)S(1)} %pad_maximum_fusion), channel_id=1, replica_groups=mesh['rep'=4,'dp'=8] {'dp'}, dimensions={0} | all-to-all | bytes 524288 | tf_op jit(solution)/shard_map/all_to_all | solution.py:216
  172.9 5.8 %all-gather.1 = f32[256,256]{1,0:T(8,128)S(1)} all-gather(f32[64,256]{1,0:T(8,128)S(1)} %convert_reduce_fusion), channel_id=3, replica_groups=mesh['rep'=4,'dp'=8] {'rep'}, dimensions={0}, use_global_device_ids=true | all-gather | bytes 327680 | tf_op jit(solution)/shard_map/all_gather | solution.py:218
  178.7 0.0 copy-done.4
  178.7 0.0 copy-done.5
  178.7 0.0 copy-done.6
  178.7 1.5 divide_subtract_fusion
  180.3 0.0 copy-done
  180.3 0.0 copy-done.1
  180.3 0.0 copy-done.2
  180.3 0.8 divide_subtract_fusion.1
  (19 shorter events, 0.2 us)
Async XLA Ops:
  7.2 81.7 %all-gather.4.cloned.1.call-start = ((), (), s32[]{:S(2)}) async-start(), calls=%async_computation.1 | async-start | bytes 1179648 | tf_op jit(solution)/shard_map/all_gather | solution.py:164
  88.8 3.7 %copy-start.3 = (bf16[512,1024]{1,0:T(8,128)(2,1)S(1)}, bf16[512,1024]{1,0:T(8,128)(2,1)}, u32[]{:S(2)}) copy-start(bf16[512,1024]{1,0:T(8,128)(2,1)} %all-gather.4.cloned.1.call-done) | copy-start | bytes 3145732
  156.4 22.3 %copy-start.4 = (f32[64,512]{1,0:T(8,128)S(1)}, f32[64,512]{1,0:T(8,128)}, u32[]{:S(2)}) copy-start(f32[64,512]{1,0:T(8,128)} %param.20) | copy-start | bytes 393220
  156.4 22.3 %copy-start.5 = (f32[64,512]{1,0:T(8,128)S(1)}, f32[64,512]{1,0:T(8,128)}, u32[]{:S(2)}) copy-start(f32[64,512]{1,0:T(8,128)} %param.21) | copy-start | bytes 393220
  156.4 22.3 %copy-start.6 = (f32[64,512]{1,0:T(8,128)S(1)}, f32[64,512]{1,0:T(8,128)}, u32[]{:S(2)}) copy-start(f32[64,512]{1,0:T(8,128)} %param.22) | copy-start | bytes 393220
  156.4 23.9 %copy-start = (f32[64,512]{1,0:T(8,128)S(1)}, f32[64,512]{1,0:T(8,128)}, u32[]{:S(2)}) copy-start(f32[64,512]{1,0:T(8,128)} %param.14) | copy-start | bytes 393220
  156.4 23.9 %copy-start.1 = (f32[64,512]{1,0:T(8,128)S(1)}, f32[64,512]{1,0:T(8,128)}, u32[]{:S(2)}) copy-start(f32[64,512]{1,0:T(8,128)} %param.15) | copy-start | bytes 393220
  156.4 23.9 %copy-start.2 = (f32[64,512]{1,0:T(8,128)S(1)}, f32[64,512]{1,0:T(8,128)}, u32[]{:S(2)}) copy-start(f32[64,512]{1,0:T(8,128)} %param.16) | copy-start | bytes 393220
Sparse Core Ops, SparseCore 0:
  10.7 43.0 all-gather.3

commit v2 on v1

--- a/solution.py
+++ b/solution.py
@@ -154,15 +154,31 @@
         ]
     )
     packed = jnp.concatenate([cotangent, pieces.astype(BF16).reshape(-1, embed_dim)], axis=0)
-    packed_all = lax.all_gather(packed, ("rep", "dp"), axis=0, tiled=False)
 
     column = jnp.arange(R * D3, dtype=jnp.int32)
     reorder = ((column[:, None] % D3) * R + column[:, None] // D3 == column[None, :]).astype(F32)
     last_wide = jnp.dot(
         last_core.astype(BF16), reorder.astype(BF16), preferred_element_type=F32
     ).astype(BF16)
-    cores = lax.all_gather(
-        jnp.concatenate([first_core.astype(BF16), last_wide], axis=1), "dp", axis=0, tiled=True
+    local_cores = jnp.concatenate([first_core.astype(BF16), last_wide], axis=1)
+    tiles = (D1 + D3) // rep_count
+    share = lax.dynamic_slice_in_dim(local_cores, lax.axis_index("rep") * (tiles * R), tiles * R, 1)
+    packed_rows = packed.shape[0]
+    message = jnp.concatenate(
+        [packed] + [share[:, n * R : (n + 1) * R] for n in range(tiles)], axis=0
+    )
+    message = jnp.broadcast_to(message[None], (dp_count, *message.shape))
+    message = lax.all_to_all(message, "dp", split_axis=0, concat_axis=0, tiled=True)
+    message = lax.all_gather(message, "rep", axis=0, tiled=False)
+    packed_all = message[:, :, :packed_rows].reshape(-1, packed_rows, embed_dim)
+    core_rows = message[:, :, packed_rows:].reshape(rep_count, dp_count, tiles, -1, R)
+    cores = jnp.concatenate(
+        [
+            core_rows[q, :, n].reshape(outer_rows, R)
+            for q in range(rep_count)
+            for n in range(tiles)
+        ],
+        axis=1,
     )
 
     blocks = packed_all.shape[0]

time: 190 us -> 157 us (0.83)
  blocking collectives: 87.6 us -> 38.2 us
  waiting for transfers between devices: 0.02 us -> 16.3 us
  local copies, waits for them, and re-layouts: 0.8 us -> 3.09 us
    all_gather x1 -> x0, blocking collectives: 71.2 us -> none  [local(): packed_all = lax.all_gather(packed, ('rep', 'dp'), axis=0, tiled=False)]
    all_to_all x0 -> x1, blocking collectives: none -> 17.8 us  [local(): lax.all_to_all(message, 'dp', split_axis=0, concat_axis=0, tiled=True)]
    all_gather x1, waiting for transfers between devices: 0.01 us -> 16.3 us  [local(): message = lax.all_gather(message, 'rep', axis=0, tiled=False)]
    all_to_all x1, blocking collectives: 10.6 us -> 14.6 us  [local(): lax.all_to_all(partial, 'dp', split_axis=0, concat_axis=0, tiled=True)]
    slice x1 -> x4, local copies, waits for them, and re-layouts: 0.09 us -> 2.35 us  [the longest x1 1.3 us: local(): message[:, :, packed_rows:].reshape(rep_count, dp_count, tiles, -1, R)]
  transfers between devices with their start and end apart: 1 -> 1, of which waited for: 0 -> 1; matrix products, arithmetic and copies ran while one was open for 4% -> 0% of each run, Pallas kernels for 0% -> 0%
where the time goes in v2:
time: 157 us; the launch traced here: 155 us
  Pallas kernels  61.4 us (39%)
  blocking collectives  38.2 us (24%)
  waiting for transfers between devices  16.3 us (10%)
  matrix products  15.3 us (10%)
  between operations  14.3 us (9%)
  other arithmetic  6.88 us (4%)
  local copies, waits for them, and re-layouts  3.09 us (2%)
    pallas_call x1, Pallas kernels, mid_step(): pl.pallas_call(lambda *refs: mid_kernel(group, slots, *refs), grid=(rows...  61.4 us
    all_to_all x1, blocking collectives, local(): lax.all_to_all(message, 'dp', split_axis=0, concat_axis=0, tiled=True)  17.8 us
    all_gather x1, waiting for transfers between devices, local(): message = lax.all_gather(message, 'rep', axis=0, tiled=False)  16.3 us
    all_to_all x1, blocking collectives, local(): lax.all_to_all(partial, 'dp', split_axis=0, concat_axis=0, tiled=True)  14.6 us
    all_gather x1, blocking collectives, local(): whole = lax.all_gather(summed, 'rep', axis=0, tiled=False)  5.79 us
    dot_general x2, matrix products, contract(): lax.dot_general(left, right, (((left_dim,), (right_dim,)), ((), ())), pre...  5.72 us
  transfers between devices with their start and end apart: 1, of which 1 were waited for; matrix products, arithmetic and copies ran while one was open for 0% of the time, Pallas kernels for 0%

profile of v2, /device:TPU:0, one launch (start us, length us, event | category | flops | bytes accessed | tf_op | source)
XLA Modules:
  0.0 155.4 jit_solution(15740171065720518339)
XLA Ops:
  7.2 0.0 all-gather.4.cloned.1.call-start
  7.2 0.8 select_reduce_fusion
  8.0 0.1 convert_reduce_fusion.1
  8.1 0.7 fusion.75
  8.9 0.7 convert_bitcast_fusion
  9.6 0.9 convert_element_type.60
  10.5 1.2 fusion.15
  11.7 0.7 pad_maximum_fusion.2
  12.5 17.8 %all_to_all.10 = bf16[8,152,128]{2,1,0:T(8,128)(2,1)} all-to-all(bf16[8,152,128]{2,1,0:T(8,128)(2,1)S(1)} %broadcast_in_dim.66), channel_id=1, replica_groups=mesh['rep'=4,'dp'=8] {'dp'}, dimensions={0} | all-to-all | bytes 622592 | tf_op jit(solution)/shard_map/all_to_all | solution.py:171
  30.3 0.0 all-gather.4.cloned.1.call-update
  30.3 0.1 add.204
  30.4 16.3 %all-gather.4.cloned.1.call-done = bf16[32,152,128]{2,1,0:T(8,128)(2,1)} async-done(((bf16[8,152,128]{2,1,0:T(8,128)(2,1)}), bf16[32,152,128]{2,1,0:T(8,128)(2,1)}) %all-gather.4.cloned.1.call-update) | async-done | bytes 1245200 | tf_op jit(solution)/shard_map/all_gather | solution.py:172
  46.6 1.0 slice.110
  47.6 1.3 slice.117
  48.9 0.1 reshape.278
  49.0 0.1 fusion.85
  49.1 0.1 fusion.52
  49.2 1.8 %fusion.17 = (s32[32,32]{1,0:T(8,128)S(1)}, s32[32,32]{1,0:T(8,128)S(1)}, s32[32,32]{1,0:T(8,128)S(1)}) fusion(s32[32,256]{1,0:T(8,128)S(1)} %fusion.52, s32[32,256]{1,0:T(8,128)S(1)} %bitcast.65, s32[32]{0:T(128)S(1)} %iota_add_fusion), kind=kLoop, calls=%fused_computation.24 | loop fusion | flops 1831936 | bytes 77952 | tf_op jit(solution)/shard_map/reduce_min | solution.py:196
  51.0 0.1 maximum_shift-right-logical_fusion.1
  51.1 0.1 fusion.84
  51.2 0.1 div.92
  51.3 0.1 ne.238
  51.4 0.1 ge.27
  51.5 0.1 ne.234
  51.5 0.1 div.95
  51.6 0.1 rem.187
  51.7 1.8 %fusion.7.refs_1_ = bf16[2048,128]{1,0:T(8,128)(2,1)} fusion(bf16[512,128]{1,0:T(8,128)(2,1)S(1)} %bitcast.66, s32[2048]{0:T(1024)S(1)} %get-tuple-element.61), kind=kOutput, calls=%fused_computation.10 | convolution fusion | flops 269746176 | bytes 663552 | tf_op jit(solution)/shard_map/dot_general | solution.py:214
  53.5 2.6 %fusion.5.refs_2_ = bf16[2048,512]{1,0:T(8,128)(2,1)} fusion(s32[2048]{0:T(1024)S(1)} %get-tuple-element.59, bf16[512,128]{1,0:T(8,128)(2,1)S(1)} %bitcast.61, bf16[512,128]{1,0:T(8,128)(2,1)S(1)} %bitcast.62, bf16[512,128]{1,0:T(8,128)(2,1)S(1)} %bitcast.63, bf16[512,128]{1,0:T(8,128)(2,1)S(1)} %bitcast.64), kind=kOutput, calls=%fused_computation.8 | convolution fusion | flops 1077936128 | bytes 2629632 | tf_op jit(solution)/shard_map/dot_general | solution.py:217
  56.0 2.5 %fusion.6.refs_3_ = bf16[2048,512]{1,0:T(8,128)(2,1)} fusion(s32[2048]{0:T(1024)S(1)} %get-tuple-element.60, bf16[512,128]{1,0:T(8,128)(2,1)S(1)} %bitcast.58, bf16[512,128]{1,0:T(8,128)(2,1)S(1)} %bitcast.59, bf16[512,128]{1,0:T(8,128)(2,1)S(1)} %bitcast.60, bf16[512,128]{1,0:T(8,128)(2,1)S(1)} %bitcast.57), kind=kOutput, calls=%fused_computation.9 | convolution fusion | flops 1077936128 | bytes 2629632 | tf_op jit(solution)/shard_map/dot_general | solution.py:218
  58.5 61.4 %shard_map.205 = (f32[32,131072]{1,0:T(8,128)}, f32[32,131072]{1,0:T(8,128)}, f32[32,131072]{1,0:T(8,128)}, f32[2048,128]{1,0:T(8,128)}, f32[2048,128]{1,0:T(8,128)}) custom-call(s32[1]{0:T(128)} %bitcast.7.refs_0_, bf16[2048,128]{1,0:T(8,128)(2,1)} %fusion.7.refs_1_, bf16[2048,512]{1,0:T(8,128)(2,1)} %fusion.5.refs_2_, bf16[2048,512]{1,0:T(8,128)(2,1)} %fusion.6.refs_3_, ...), custom_call_target="tpu_custom_call" | custom-call | tf_op jit(solution)/shard_map/pallas_call | solution.py:108
  119.9 0.0 copy-start.3
  119.9 0.0 copy-start.4
  119.9 0.0 copy-start.5
  119.9 0.0 copy-start
  119.9 0.0 copy-start.1
  120.0 0.0 copy-start.2
  120.0 2.9 %fusion.13 = bf16[512,128]{1,0:T(8,128)(2,1)S(1)} fusion(s32[2048]{0:T(1024)S(1)} %get-tuple-element.59, f32[2048,128]{1,0:T(8,128)} %get-tuple-element.14), kind=kOutput, calls=%fused_computation.19 | convolution fusion | flops 269811712 | bytes 1187840 | tf_op jit(solution)/shard_map/dot_general | solution.py:36
  122.9 2.8 %fusion.14 = bf16[512,128]{1,0:T(8,128)(2,1)S(1)} fusion(s32[2048]{0:T(1024)S(1)} %get-tuple-element.60, f32[2048,128]{1,0:T(8,128)} %get-tuple-element.15), kind=kOutput, calls=%fused_computation.20 | convolution fusion | flops 269811712 | bytes 1187840 | tf_op jit(solution)/shard_map/dot_general | solution.py:36
  125.7 14.6 %all_to_all.11 = bf16[8,64,256]{2,1,0:T(8,128)(2,1)S(1)} all-to-all(bf16[8,64,256]{2,1,0:T(8,128)(2,1)S(1)} %pad_maximum_fusion), channel_id=1, replica_groups=mesh['rep'=4,'dp'=8] {'dp'}, dimensions={0} | all-to-all | bytes 524288 | tf_op jit(solution)/shard_map/all_to_all | solution.py:232
  140.4 5.8 %all-gather.1 = f32[256,256]{1,0:T(8,128)S(1)} all-gather(f32[64,256]{1,0:T(8,128)S(1)} %convert_reduce_fusion), channel_id=3, replica_groups=mesh['rep'=4,'dp'=8] {'rep'}, dimensions={0}, use_global_device_ids=true | all-gather | bytes 327680 | tf_op jit(solution)/shard_map/all_gather | solution.py:234
  146.2 0.0 copy-done.3
  146.2 0.0 copy-done.4
  146.2 0.0 copy-done.5
  146.2 1.5 divide_subtract_fusion
  147.8 0.0 copy-done
  147.8 0.0 copy-done.1
  147.8 0.0 copy-done.2
  147.8 0.8 divide_subtract_fusion.1
  (22 shorter events, 0.3 us)
Async XLA Ops:
  7.2 39.5 %all-gather.4.cloned.1.call-start = ((), (), s32[]{:S(2)}) async-start(), calls=%async_computation.2 | async-start | bytes 1556480 | tf_op jit(solution)/shard_map/all_gather | solution.py:172
  119.9 26.3 %copy-start.3 = (f32[64,512]{1,0:T(8,128)S(1)}, f32[64,512]{1,0:T(8,128)}, u32[]{:S(2)}) copy-start(f32[64,512]{1,0:T(8,128)} %param.20) | copy-start | bytes 393220
  119.9 26.3 %copy-start.4 = (f32[64,512]{1,0:T(8,128)S(1)}, f32[64,512]{1,0:T(8,128)}, u32[]{:S(2)}) copy-start(f32[64,512]{1,0:T(8,128)} %param.21) | copy-start | bytes 393220
  119.9 26.3 %copy-start.5 = (f32[64,512]{1,0:T(8,128)S(1)}, f32[64,512]{1,0:T(8,128)}, u32[]{:S(2)}) copy-start(f32[64,512]{1,0:T(8,128)} %param.22) | copy-start | bytes 393220
  119.9 27.9 %copy-start = (f32[64,512]{1,0:T(8,128)S(1)}, f32[64,512]{1,0:T(8,128)}, u32[]{:S(2)}) copy-start(f32[64,512]{1,0:T(8,128)} %param.14) | copy-start | bytes 393220
  119.9 27.9 %copy-start.1 = (f32[64,512]{1,0:T(8,128)S(1)}, f32[64,512]{1,0:T(8,128)}, u32[]{:S(2)}) copy-start(f32[64,512]{1,0:T(8,128)} %param.15) | copy-start | bytes 393220
  120.0 27.8 %copy-start.2 = (f32[64,512]{1,0:T(8,128)S(1)}, f32[64,512]{1,0:T(8,128)}, u32[]{:S(2)}) copy-start(f32[64,512]{1,0:T(8,128)} %param.16) | copy-start | bytes 393220
Sparse Core Ops, SparseCore 0:
  30.4 16.1 all-gather.3
